TPU v7x, 256 devices: a whole 4x4x8 slice. The times are simulated.
256 devices in a mesh: row: 16 (over x, y), col: 16 (over z, core).
Axes of the slice: x: 4, y: 4, z: 8, core: 2. Of those that a mesh axis runs over, the one named last changes fastest.
Arguments:
- source: float32 [8, 8192, 4096], P(None, 'col', 'row'), may hold values from -6 to 6
- pole_x: float32 [8, 4], replicated, may hold values from 0.95 to 1, as said below
- weight_x: float32 [8, 4], replicated, may hold values from 0.15 to 0.4
- pole_y: float32 [8, 4], replicated, may hold values from 0.95 to 1, as said below
- weight_y: float32 [8, 4], replicated, may hold values from 0.15 to 0.4
Outputs:
- coefficient: float32 [8, 8192, 4096], P(None, 'col', 'row')
Inputs may be any that keep to these rules, and one draw needn't show every extreme that they name: `pole_x`: each pole is below one. `pole_y`: each pole is below one.
All inputs are finite; a program needn't handle non-finite values.
Results may differ from a plain program's by a relative error of at most 0.0003.
Values sent between devices are 32-bit elements; how exact they have to be, the bound alone decides.
A program may use at most 128 MiB of HBM per device.

v0:
```python
import jax
import jax.numpy as jnp
from jax import lax
from jax.sharding import PartitionSpec as P

highest = lax.Precision.HIGHEST


def prefix(value, axis, join, neutral, backward):
    count, mine = (lax.axis_size(axis), lax.axis_index(axis))
    pieces = jax.tree.map(lambda part: lax.all_gather(part, axis), value)
    if backward:
        pieces = jax.tree.map(lambda part: part[::-1], pieces)
        mine = count - 1 - mine
    subtotal = jax.tree.map(
        lambda part, zero: jnp.full_like(part, 0) + jnp.asarray(zero, part.dtype), value, neutral
    )

    def lap(position, subtotal):
        longer = join(subtotal, jax.tree.map(lambda part: part[position], pieces))
        return jax.tree.map(lambda new, old: jnp.where(position < mine, new, old), longer, subtotal)

    return lax.fori_loop(0, count - 1, lap, subtotal)


def block_tables(pole_values, weights, block_len, forward):
    log_pole = jnp.log(pole_values)
    places = jnp.arange(block_len, dtype=jnp.float32)
    if forward:
        gain_rate = jnp.sqrt(1.0 - pole_values * pole_values)
        offset = places[:, None] - places[None, :]
        state_expo = block_len - 1.0 - places
        carry_expo = places + 1.0
    else:
        gain_rate = 1.0 - pole_values
        offset = places[None, :] - places[:, None]
        state_expo = places
        carry_expo = block_len - places
    inside = offset >= 0.0
    decays = jnp.exp(log_pole[:, :, None, None] * jnp.maximum(offset, 0.0))
    decays = jnp.where(inside, decays, 0.0)
    matrix = jnp.einsum("lk,lkab->lab", weights * gain_rate, decays, precision=highest)
    state_map = gain_rate[:, :, None] * jnp.exp(log_pole[:, :, None] * state_expo[None, None, :])
    carry_map = weights[:, None, :] * jnp.exp(log_pole[:, None, :] * carry_expo[None, :, None])
    return (matrix, state_map, carry_map)


def chain_tables(pole_values, block_len, blocks, forward):
    step_log = jnp.log(pole_values) * block_len
    positions = jnp.arange(blocks, dtype=jnp.float32)
    if forward:
        distance = positions[:, None] - 1.0 - positions[None, :]
        summary_expo = blocks - 1.0 - positions
        entry_expo = positions
    else:
        distance = positions[None, :] - 1.0 - positions[:, None]
        summary_expo = positions
        entry_expo = blocks - 1.0 - positions
    spread = jnp.exp(step_log[:, :, None, None] * jnp.maximum(distance, 0.0))
    spread = jnp.where(distance >= 0.0, spread, 0.0)
    summary_w = jnp.exp(step_log[:, :, None] * summary_expo[None, None, :])
    entry_w = jnp.exp(step_log[:, :, None] * entry_expo[None, None, :])
    return (spread, summary_w, entry_w)


def line_local(field_in, pole_values, weights, line_dim, forward):
    levels, middle_size, inner_size = field_in.shape
    length = field_in.shape[line_dim]
    block_len = 128
    blocks = length // block_len
    matrix, state_map, carry_map = block_tables(pole_values, weights, block_len, forward)
    spread, summary_w, entry_w = chain_tables(pole_values, block_len, blocks, forward)
    if line_dim == 2:
        blocked = field_in.reshape(levels, middle_size, blocks, block_len)
        local_part = jnp.einsum("lab,lmcb->lmca", matrix, blocked, precision=highest)
        states = jnp.einsum("lkb,lmcb->lckm", state_map, blocked, precision=highest)
    else:
        blocked = field_in.reshape(levels, blocks, block_len, inner_size)
        local_part = jnp.einsum("lab,lcbm->lcam", matrix, blocked, precision=highest)
        states = jnp.einsum("lkb,lcbm->lckm", state_map, blocked, precision=highest)
    inner_carry = jnp.einsum("lkcd,ldkm->lckm", spread, states, precision=highest)
    summary = jnp.einsum("lkc,lckm->lkm", summary_w, states, precision=highest)
    return (local_part, inner_carry, summary, (carry_map, entry_w))


def line_finish(local_part, inner_carry, tables, incoming, line_dim, shape_out):
    carry_map, entry_w = tables
    carries = inner_carry + jnp.swapaxes(entry_w, 1, 2)[:, :, :, None] * incoming[:, None, :, :]
    if line_dim == 2:
        fixed = local_part + jnp.einsum("lak,lckm->lmca", carry_map, carries, precision=highest)
    else:
        fixed = local_part + jnp.einsum("lak,lckm->lcam", carry_map, carries, precision=highest)
    return fixed.reshape(shape_out)


def join_segments(earlier, later_part):
    return (earlier[0] * later_part[0], later_part[0] * earlier[1] + later_part[1])


def on_device(source, pole_x, weight_x, pole_y, weight_y):
    levels, rows_here, cols_here = source.shape
    pole_count = pole_x.shape[1]
    line_rows = lax.all_to_all(source, "row", split_axis=1, concat_axis=2, tiled=True)
    zero_in = jnp.zeros((levels, pole_count, line_rows.shape[1]), jnp.float32)
    local_part, inner_carry, summary, tables = line_local(line_rows, pole_x, weight_x, 2, True)
    along_x = line_finish(local_part, inner_carry, tables, zero_in, 2, line_rows.shape)
    local_part, inner_carry, summary, tables = line_local(along_x, pole_x, weight_x, 2, False)
    smooth_lines = line_finish(local_part, inner_carry, tables, zero_in, 2, line_rows.shape)
    smooth_x = lax.all_to_all(smooth_lines, "row", split_axis=2, concat_axis=1, tiled=True)
    decay_y = jnp.exp(jnp.log(pole_y) * rows_here)[:, :, None]
    identity = (jnp.ones_like(decay_y), jnp.zeros((levels, pole_count, cols_here), jnp.float32))
    local_part, inner_carry, summary, tables = line_local(smooth_x, pole_y, weight_y, 1, True)
    from_below = prefix((decay_y, summary), "col", join_segments, identity, False)[1]
    along_y = line_finish(local_part, inner_carry, tables, from_below, 1, smooth_x.shape)
    local_part, inner_carry, summary, tables = line_local(along_y, pole_y, weight_y, 1, False)
    from_above = prefix((decay_y, summary), "col", join_segments, identity, True)[1]
    smooth_y = line_finish(local_part, inner_carry, tables, from_above, 1, smooth_x.shape)
    return jnp.exp(smooth_y)


def solution(mesh):
    return jax.shard_map(
        on_device,
        mesh=mesh,
        in_specs=(P(None, "col", "row"), P(), P(), P(), P()),
        out_specs=P(None, "col", "row"),
        check_vma=False,
    )
```

profile of v0, /device:TPU:1, one launch (start us, length us, event | category | flops | bytes accessed | tf_op | source)
XLA Modules:
  0.0 365.1 jit_solution(4943154217428443616)
XLA Ops:
  0.0 6.6 %copy.97 = f32[8,512,256]{2,0,1:T(8,128)} copy(f32[8,512,256]{2,1,0:T(8,128)} %param.9) | data formatting | bytes 8388608 | tf_op args[0]
  6.6 8.0 %all-to-all-start = ((f32[8,512,256]{2,0,1:T(8,128)}), f32[8,512,256]{2,0,1:T(8,128)}, u32[]{:S(2)}, u32[]{:S(2)}) async-start(f32[8,512,256]{2,0,1:T(8,128)} %copy.97), calls=%async_computation | async-start | bytes 8388608 | tf_op jit(solution)/shard_map/all_to_all | solution.py:103
  15.7 2.6 exponential_select_fusion.2
  18.2 4.3 %fusion.10 = f32[8,1,128,128]{3,1,2,0:T(1,128)S(1)} fusion(f32[8,4,1,1]{1,2,3,0:T(1,128)S(1)} %copy.137, f32[8,4,128,128]{3,2,1,0:T(8,128)S(1)} %get-tuple-element.293), kind=kOutput, calls=%fused_computation.19 | convolution fusion | flops 6291456 | bytes 2621568 | tf_op jit(solution)/shard_map/lk,lkab->lab/dot_general | solution.py:42
  22.5 4.3 %fusion.12 = f32[8,1,128,128]{3,1,2,0:T(1,128)S(1)} fusion(f32[8,4,1,1]{1,2,3,0:T(1,128)S(1)} %copy.131, f32[8,4,128,128]{3,2,1,0:T(8,128)S(1)} %get-tuple-element.295), kind=kOutput, calls=%fused_computation.21 | convolution fusion | flops 6291456 | bytes 2621568 | tf_op jit(solution)/shard_map/lk,lkab->lab/dot_general | solution.py:42
  26.8 48.6 %all-to-all-done = f32[8,512,256]{2,0,1:T(8,128)} async-done(((f32[8,512,256]{2,0,1:T(8,128)}), f32[8,512,256]{2,0,1:T(8,128)}, u32[]{:S(2)}, u32[]{:S(2)}) %all-to-all-start) | async-done | bytes 4194336 | tf_op jit(solution)/shard_map/all_to_all | solution.py:103
  75.4 6.6 %copy.196 = f32[8,16,32,256]{3,1,2,0:T(8,128)} copy(f32[8,16,32,256]{3,0,2,1:T(8,128)} %bitcast.5) | data formatting | bytes 8388608 | tf_op jit(solution)/shard_map/all_to_all | solution.py:103
  82.0 4.7 %reshape.193 = f32[8,32,32,128]{3,2,1,0:T(8,128)} reshape(f32[8,32,16,256]{3,2,1,0:T(8,128)} %bitcast.185) | data formatting | bytes 8388608 | tf_op jit(solution)/shard_map/reshape | solution.py:74
  86.7 5.7 %fusion.133 = f32[8,128,32,32]{1,3,2,0:T(8,128)S(1)} fusion(f32[8,128,128,1]{2,1,3,0:T(8,128)S(1)} %bitcast.189, f32[8,32,32,128]{3,2,1,0:T(8,128)} %reshape.193), kind=kOutput, calls=%fused_computation.184 | convolution fusion | flops 1610612736 | bytes 8912896 | tf_op jit(solution)/shard_map/lab,lmcb->lmca/dot_general | solution.py:75
  92.5 16.3 %convolution_bitcast_fusion.1 = f32[8,32,4,32]{1,2,3,0:T(4,128)S(1)} fusion(f32[8,32,32,128]{3,2,1,0:T(8,128)S(1)} %copy-done.1, f32[128]{0:T(128)S(1)} %iota_subtract_fusion.9, f32[8,4]{1,0:T(8,128)S(1)} %copy.96, f32[8,4]{1,0:T(8,128)S(1)} %copy.99), kind=kOutput, calls=%fused_computation.28 | convolution fusion | flops 50339840 | bytes 4326144 | tf_op jit(solution)/shard_map/lkb,lmcb->lckm/dot_general | solution.py:76
  108.8 1.1 fusion.15
  109.9 7.2 %bitcast_add_fusion.3 = f32[8,32,32,128]{3,2,1,0:T(8,128)S(1)} fusion(f32[8,128,32,32]{1,3,2,0:T(8,128)S(1)} %fusion.133, f32[8,32,4,32]{1,3,2,0:T(8,128)S(1)} %fusion.15, f32[128]{0:T(128)S(1)} %iota_add_fusion.1, f32[8,4]{1,0:T(8,128)S(1)} %copy.96, f32[8,4]{1,0:T(8,128)S(1)} %copy.104), kind=kOutput, calls=%fused_computation.11 | convolution fusion | flops 51388416 | bytes 8520448 | tf_op jit(solution)/shard_map/lak,lckm->lmca/dot_general | solution.py:90
  117.2 16.3 %convolution_bitcast_fusion = f32[8,32,4,32]{1,2,3,0:T(4,128)S(1)} fusion(f32[8,32,32,128]{3,2,1,0:T(8,128)S(1)} %bitcast_add_fusion.3, f32[8,4]{1,0:T(8,128)S(1)} %copy.107, f32[8,4]{1,0:T(8,128)S(1)} %copy.96), kind=kOutput, calls=%fused_computation.27 | convolution fusion | flops 50339840 | bytes 4325632 | tf_op jit(solution)/shard_map/lkb,lmcb->lckm/dot_general | solution.py:76
  133.5 4.5 %fusion.134 = f32[8,32,32,128]{3,2,1,0:T(8,128)S(1)} fusion(f32[8,32,32,128]{3,2,1,0:T(8,128)S(1)} %bitcast_add_fusion.3, f32[8,128,128,1]{2,1,3,0:T(8,128)S(1)} %bitcast.187), kind=kOutput, calls=%fused_computation.185 | convolution fusion | flops 1610612736 | bytes 8912896 | tf_op jit(solution)/shard_map/lab,lmcb->lmca/dot_general | solution.py:75
  138.0 1.1 fusion.14
  139.1 8.4 %bitcast_add_fusion.2 = f32[8,32,32,128]{3,2,1,0:T(8,128)} fusion(f32[8,32,32,128]{3,2,1,0:T(8,128)S(1)} %fusion.134, f32[8,32,4,32]{1,3,2,0:T(8,128)S(1)} %fusion.14, f32[128]{0:T(128)S(1)} %iota_subtract_fusion.7, f32[8,4]{1,0:T(8,128)S(1)} %copy.96, f32[8,4]{1,0:T(8,128)S(1)} %copy.104), kind=kOutput, calls=%fused_computation.10 | convolution fusion | flops 51388416 | bytes 8520448 | tf_op jit(solution)/shard_map/lak,lckm->lmca/dot_general | solution.py:90
  147.5 9.4 %copy.162 = f32[8,32,32,128]{1,0,3,2:T(8,128)} copy(f32[8,32,32,128]{3,2,1,0:T(8,128)} %bitcast_add_fusion.2) | data formatting | bytes 8388608 | tf_op jit(solution)/shard_map/reshape | solution.py:93
  156.9 16.0 %reshape.227 = f32[16,1,65536]{2,1,0:T(1,128)} reshape(f32[4096,8,32]{2,1,0:T(8,128)} %bitcast.181) | data formatting | bytes 8388608
  172.9 10.8 %all-to-all-start.1 = ((f32[16,1,65536]{2,1,0:T(1,128)}), f32[16,1,65536]{2,1,0:T(1,128)}, u32[]{:S(2)}, u32[]{:S(2)}) async-start(f32[16,1,65536]{2,1,0:T(1,128)} %reshape.227), calls=%async_computation.1 | async-start | bytes 8388608 | tf_op jit(solution)/shard_map/all_to_all | solution.py:109
  184.2 22.2 %all-gather.3 = f32[16,8,4]{1,2,0:T(4,128)S(1)} all-gather(f32[1,8,4]{1,2,0:T(4,128)S(1)} %get-tuple-element.309), channel_id=2, replica_groups=mesh['row'=16,'col'=16] {'col'}, dimensions={0}, use_global_device_ids=true | all-gather | bytes 2176 | tf_op jit(solution)/shard_map/all_gather | solution.py:11
  206.8 6.6 %fusion.6 = f32[8,1,128,128]{3,1,2,0:T(1,128)S(1)} fusion(f32[8,4,1,1]{1,2,3,0:T(1,128)S(1)} %copy.152, f32[8,4,128,128]{3,2,1,0:T(8,128)} %get-tuple-element.294), kind=kOutput, calls=%fused_computation.15 | convolution fusion | flops 6291456 | bytes 2621568 | tf_op jit(solution)/shard_map/lk,lkab->lab/dot_general | solution.py:42
  213.4 4.7 %fusion.8 = f32[8,1,128,128]{3,1,2,0:T(1,128)S(1)} fusion(f32[8,4,1,1]{1,2,3,0:T(1,128)S(1)} %copy.143, f32[8,4,128,128]{3,2,1,0:T(8,128)S(1)} %get-tuple-element.296), kind=kOutput, calls=%fused_computation.17 | convolution fusion | flops 6291456 | bytes 2621568 | tf_op jit(solution)/shard_map/lk,lkab->lab/dot_general | solution.py:42
  218.1 16.9 %all-to-all-done.1 = f32[16,1,65536]{2,1,0:T(1,128)} async-done(((f32[16,1,65536]{2,1,0:T(1,128)}), f32[16,1,65536]{2,1,0:T(1,128)}, u32[]{:S(2)}, u32[]{:S(2)}) %all-to-all-start.1) | async-done | bytes 4194336 | tf_op jit(solution)/shard_map/all_to_all | solution.py:109
  235.0 0.6 broadcast.274
  235.5 13.8 %reduce = f32[16,65536]{1,0:T(8,128)} reduce(f32[16,1,65536]{2,1,0:T(1,128)} %all-to-all-done.1, f32[]{:T(128)} %broadcast.274), dimensions={1}, to_apply=%all_to_all.25.reduce_sub_computation | reduce | bytes 8388612 | tf_op jit(solution)/shard_map/all_to_all | solution.py:109
  249.3 15.1 %reshape.228 = f32[4096,8,32]{2,1,0:T(8,128)} reshape(f32[16,65536]{1,0:T(8,128)} %reduce) | data formatting | bytes 8388608
  264.4 11.4 %copy.112 = f32[8,16,32,256]{3,2,1,0:T(8,128)} copy(f32[8,16,32,256]{2,0,3,1:T(8,128)} %bitcast.182) | data formatting | bytes 8388608 | tf_op jit(solution)/shard_map/all_to_all | solution.py:109
  275.8 4.6 %convolution_bitcast_fusion.6 = f32[8,4,4,256]{3,2,1,0:T(4,128)S(1)} fusion(f32[8,4,128,256]{3,2,1,0:T(8,128)} %bitcast.183, f32[8,4]{1,0:T(8,128)S(1)} %copy.113, f32[8,4]{1,0:T(8,128)S(1)} %copy.115, f32[128]{0:T(128)S(1)} %iota_subtract_fusion.9), kind=kOutput, calls=%fused_computation.38 | convolution fusion | flops 50339840 | bytes 4326144 | tf_op jit(solution)/shard_map/lkb,lcbm->lckm/dot_general | solution.py:80
  280.4 8.3 %fusion.135 = f32[8,4,256,128]{3,2,1,0:T(8,128)} fusion(f32[8,4,128,256]{3,2,1,0:T(8,128)S(1)} %bitcast.184, f32[8,128,128,1]{2,1,3,0:T(8,128)S(1)} %bitcast.188), kind=kOutput, calls=%fused_computation.186 | convolution fusion | flops 1610612736 | bytes 8912896 | tf_op jit(solution)/shard_map/lab,lcbm->lcam/dot_general | solution.py:79
  288.7 0.4 fusion.44
  289.1 26.7 %all-gather.1 = f32[128,4,256]{2,1,0:T(4,128)S(1)} all-gather(f32[8,4,256]{2,1,0:T(4,128)S(1)} %bitcast.193), channel_id=3, replica_groups=mesh['row'=16,'col'=16] {'col'}, dimensions={0}, use_global_device_ids=true | all-gather | bytes 557056 | tf_op jit(solution)/shard_map/all_gather | solution.py:11
  315.8 3.3 while.28
  316.1 0.1 fusion.154
  316.3 0.1 fusion.154
  316.5 0.1 fusion.154
  316.7 0.1 fusion.154
  316.9 0.1 fusion.154
  317.1 0.1 fusion.154
  317.3 0.1 fusion.154
  319.1 0.4 fusion.17
  319.6 8.5 %convolution_add_fusion = f32[8,4,256,128]{3,2,1,0:T(8,128)S(1)} fusion(f32[8,4,256,128]{3,2,1,0:T(8,128)} %fusion.135, f32[8,4,4,256]{3,1,2,0:T(4,128)S(1)} %fusion.17, f32[8,4]{1,0:T(8,128)S(1)} %copy.113, f32[8,4]{1,0:T(8,128)S(1)} %copy.122, f32[128]{0:T(128)S(1)} %iota_add_fusion.1), kind=kOutput, calls=%fused_computation.14 | convolution fusion | flops 51388416 | bytes 8520448 | tf_op jit(solution)/shard_map/lak,lckm->lcam/dot_general | solution.py:92
  328.1 3.6 fusion.18
  331.7 5.9 %fusion.4 = f32[8,4,256,128]{2,3,1,0:T(8,128)} fusion(f32[8,128,128,1]{2,1,3,0:T(8,128)S(1)} %bitcast.186, f32[8,4,256,128]{3,2,1,0:T(8,128)S(1)} %convolution_add_fusion), kind=kOutput, calls=%fused_computation.8 | convolution fusion | flops 1610612736 | bytes 8912896 | tf_op jit(solution)/shard_map/lab,lcbm->lcam/dot_general | solution.py:79
  337.6 0.4 fusion.41
  338.0 15.9 %all-gather.2 = f32[128,4,256]{2,1,0:T(4,128)S(1)} all-gather(f32[8,4,256]{2,1,0:T(4,128)S(1)} %bitcast.194), channel_id=4, replica_groups=mesh['row'=16,'col'=16] {'col'}, dimensions={0}, use_global_device_ids=true | all-gather | bytes 557056 | tf_op jit(solution)/shard_map/all_gather | solution.py:11
  353.9 3.1 while.29
  357.1 0.4 fusion.16
  357.5 7.5 %add_exponential_fusion = f32[8,4,256,128]{2,3,1,0:T(8,128)} fusion(f32[8,4,256,128]{2,3,1,0:T(8,128)} %fusion.4, f32[8,4,4,256]{3,1,2,0:T(4,128)S(1)} %fusion.16, f32[8,4]{1,0:T(8,128)S(1)} %copy.113, f32[8,4]{1,0:T(8,128)S(1)} %copy.122, f32[128]{0:T(128)S(1)} %iota_subtract_fusion.7), kind=kOutput, calls=%fused_computation.13 | convolution fusion | flops 51388416 | bytes 8520448 | tf_op jit(solution)/shard_map/lak,lckm->lcam/dot_general | solution.py:92
  (133 shorter events, 6.7 us)
Async XLA Ops:
  6.6 8.0 %copy-start.3 = (f32[8,4]{0,1:T(4,128)S(1)}, f32[8,4]{0,1:T(4,128)}, u32[]{:S(2)}) copy-start(f32[8,4]{0,1:T(4,128)} %param.11) | copy-start | bytes 388
  6.6 8.1 %copy-start.5 = (f32[8,4]{0,1:T(4,128)S(1)}, f32[8,4]{0,1:T(4,128)}, u32[]{:S(2)}) copy-start(f32[8,4]{0,1:T(4,128)} %param.10) | copy-start | bytes 388
  6.6 8.6 %copy-start.2 = (f32[8,4]{0,1:T(4,128)S(1)}, f32[8,4]{0,1:T(4,128)}, u32[]{:S(2)}) copy-start(f32[8,4]{0,1:T(4,128)} %param.13) | copy-start | bytes 388
  6.6 8.6 %copy-start.4 = (f32[8,4]{0,1:T(4,128)S(1)}, f32[8,4]{0,1:T(4,128)}, u32[]{:S(2)}) copy-start(f32[8,4]{0,1:T(4,128)} %param.12) | copy-start | bytes 388
  6.6 68.7 %all-to-all-start = ((f32[8,512,256]{2,0,1:T(8,128)}), f32[8,512,256]{2,0,1:T(8,128)}, u32[]{:S(2)}, u32[]{:S(2)}) async-start(f32[8,512,256]{2,0,1:T(8,128)} %copy.97), calls=%async_computation | async-start | bytes 8388608 | tf_op jit(solution)/shard_map/all_to_all | solution.py:103
  86.7 5.8 %copy-start.1 = (f32[8,32,32,128]{3,2,1,0:T(8,128)S(1)}, f32[8,32,32,128]{3,2,1,0:T(8,128)}, u32[]{:S(2)}) copy-start(f32[8,32,32,128]{3,2,1,0:T(8,128)} %reshape.193) | copy-start | bytes 12582916
  172.9 62.0 %all-to-all-start.1 = ((f32[16,1,65536]{2,1,0:T(1,128)}), f32[16,1,65536]{2,1,0:T(1,128)}, u32[]{:S(2)}, u32[]{:S(2)}) async-start(f32[16,1,65536]{2,1,0:T(1,128)} %reshape.227), calls=%async_computation.1 | async-start | bytes 8388608 | tf_op jit(solution)/shard_map/all_to_all | solution.py:109
  275.8 4.6 %copy-start = (f32[8,16,32,256]{3,2,1,0:T(8,128)S(1)}, f32[8,16,32,256]{3,2,1,0:T(8,128)}, u32[]{:S(2)}) copy-start(f32[8,16,32,256]{3,2,1,0:T(8,128)} %copy.112) | copy-start | bytes 12582916
where the time goes:
time: 369 us; the launch traced here: 365 us
  matrix products  120 us (33%)
  local copies, waits for them, and re-layouts  74.4 us (20%)
  waiting for transfers between devices  65.5 us (18%)
  blocking collectives  64.9 us (18%)
  other arithmetic  19.7 us (5%)
  starting transfers between devices  18.8 us (5%)
    all_gather x3, blocking collectives, prefix(): pieces = jax.tree.map(lambda part: lax.all_gather(part, axis), value)  64.9 us
    all_to_all x1, waiting for transfers between devices, on_device(): lax.all_to_all(source, 'row', split_axis=1, concat_axis=2, tiled=True)  48.6 us
    unnamed x18, local copies, waits for them, and re-layouts  37.9 us
    dot_general x2, matrix products, line_local(): states = jnp.einsum('lkb,lmcb->lckm', state_map, blocked, precision=highest)  32.6 us
    dot_general x4, matrix products, block_tables(): jnp.einsum('lk,lkab->lab', weights * gain_rate, decays, precision=highest)  19.8 us
    all_to_all x1, waiting for transfers between devices, on_device(): lax.all_to_all(smooth_lines, 'row', split_axis=2, concat_axis=1, tiled=True)  16.9 us
    dot_general x2, matrix products, line_finish(): jnp.einsum('lak,lckm->lcam', carry_map, carries, precision=highest)  16 us
    dot_general x2, matrix products, line_finish(): jnp.einsum('lak,lckm->lmca', carry_map, carries, precision=highest)  15.7 us
  transfers between devices with their start and end apart: 2, of which 2 were waited for; matrix products, arithmetic and copies ran while one was open for 7% of the time, Pallas kernels for 0%

commit v1 on v0

--- a/solution.py
+++ b/solution.py
@@ -4,6 +4,18 @@
 from jax.sharding import PartitionSpec as P
 
 highest = lax.Precision.HIGHEST
+
+
+def exchange_directly(array, axis, split, join):
+    ways, here = (lax.axis_size(axis), lax.axis_index(axis))
+    width = array.shape[split] // ways
+    turned = jnp.roll(array, -here * width, axis=split)
+    got = [lax.slice_in_dim(turned, 0, width, axis=split)]
+    for far in range(1, ways):
+        sent = lax.slice_in_dim(turned, far * width, (far + 1) * width, axis=split)
+        got.append(lax.ppermute(sent, axis, [(d, (d + far) % ways) for d in range(ways)]))
+    line = jnp.concatenate(got[::-1], axis=join)
+    return jnp.roll(line, (here + 1) * got[0].shape[join], axis=join)
 
 
 def prefix(value, axis, join, neutral, backward):
@@ -106,7 +118,7 @@
     along_x = line_finish(local_part, inner_carry, tables, zero_in, 2, line_rows.shape)
     local_part, inner_carry, summary, tables = line_local(along_x, pole_x, weight_x, 2, False)
     smooth_lines = line_finish(local_part, inner_carry, tables, zero_in, 2, line_rows.shape)
-    smooth_x = lax.all_to_all(smooth_lines, "row", split_axis=2, concat_axis=1, tiled=True)
+    smooth_x = exchange_directly(smooth_lines, "row", 2, 1)
     decay_y = jnp.exp(jnp.log(pole_y) * rows_here)[:, :, None]
     identity = (jnp.ones_like(decay_y), jnp.zeros((levels, pole_count, cols_here), jnp.float32))
     local_part, inner_carry, summary, tables = line_local(smooth_x, pole_y, weight_y, 1, True)

time: 369 us -> 353 us (0.957)
  local copies, waits for them, and re-layouts: 74.4 us -> 37.1 us
  starting transfers between devices: 18.8 us -> 55.2 us
  other arithmetic: 19.7 us -> 10.4 us
  matrix products: 120 us -> 112 us
    ppermute x0 -> x15, starting transfers between devices: none -> 47.2 us  [exchange_directly(): lax.ppermute(sent, axis, [(d, (d + far) % ways) for d in range(ways)])]
    unnamed x18 -> x81, local copies, waits for them, and re-layouts: 37.9 us -> 12.4 us
    ppermute x0 -> x15, waiting for transfers between devices: none -> 24.3 us  [exchange_directly(): lax.ppermute(sent, axis, [(d, (d + far) % ways) for d in range(ways)])]
    all_to_all x1 -> x0, waiting for transfers between devices: 16.9 us -> none  [on_device(): lax.all_to_all(smooth_lines, 'row', split_axis=2, concat_axis=1, tiled=True)]
    all_to_all x1 -> x0, other arithmetic: 13.8 us -> none  [on_device(): lax.all_to_all(smooth_lines, 'row', split_axis=2, concat_axis=1, tiled=True)]
    all_to_all x2 -> x0, local copies, waits for them, and re-layouts: 12 us -> none  [on_device(): lax.all_to_all(smooth_lines, 'row', split_axis=2, concat_axis=1, tiled=True)]
    all_to_all x1 -> x0, starting transfers between devices: 10.8 us -> none  [on_device(): lax.all_to_all(smooth_lines, 'row', split_axis=2, concat_axis=1, tiled=True)]
    all_to_all x1, waiting for transfers between devices: 48.6 us -> 38 us  [on_device(): lax.all_to_all(source, 'row', split_axis=1, concat_axis=2, tiled=True)]
  transfers between devices with their start and end apart: 2 -> 16, of which waited for: 2 -> 7; matrix products, arithmetic and copies ran while one was open for 7% -> 7% of each run, Pallas kernels for 0% -> 0%
where the time goes in v1:
time: 353 us; the launch traced here: 346 us
  matrix products  112 us (32%)
  blocking collectives  67 us (19%)
  waiting for transfers between devices  62.3 us (18%)
  starting transfers between devices  55.2 us (16%)
  local copies, waits for them, and re-layouts  37.1 us (11%)
  other arithmetic  10.4 us (3%)
    all_gather x3, blocking collectives, prefix(): pieces = jax.tree.map(lambda part: lax.all_gather(part, axis), value)  67 us
    ppermute x15, starting transfers between devices, exchange_directly(): lax.ppermute(sent, axis, [(d, (d + far) % ways) for d in range(ways)])  47.2 us
    all_to_all x1, waiting for transfers between devices, on_device(): lax.all_to_all(source, 'row', split_axis=1, concat_axis=2, tiled=True)  38 us
    dot_general x2, matrix products, line_local(): states = jnp.einsum('lkb,lmcb->lckm', state_map, blocked, precision=highest)  32.6 us
    ppermute x15, waiting for transfers between devices, exchange_directly(): lax.ppermute(sent, axis, [(d, (d + far) % ways) for d in range(ways)])  24.3 us
    dot_general x4, matrix products, block_tables(): jnp.einsum('lk,lkab->lab', weights * gain_rate, decays, precision=highest)  17.5 us
    dot_general x2, matrix products, line_finish(): jnp.einsum('lak,lckm->lmca', carry_map, carries, precision=highest)  15.4 us
    dot_general x2, matrix products, line_finish(): jnp.einsum('lak,lckm->lcam', carry_map, carries, precision=highest)  14.2 us
  transfers between devices with their start and end apart: 16, of which 7 were waited for; matrix products, arithmetic and copies ran while one was open for 7% of the time, Pallas kernels for 0%

profile of v1, /device:TPU:1, one launch (start us, length us, event | category | flops | bytes accessed | tf_op | source)
XLA Modules:
  0.0 346.2 jit_solution(1017351792303578551)
XLA Ops:
  0.0 6.6 %copy.63 = f32[8,512,256]{2,0,1:T(8,128)} copy(f32[8,512,256]{2,1,0:T(8,128)} %param.9) | data formatting | bytes 8388608 | tf_op args[0]
  6.6 8.0 %all-to-all-start = ((f32[8,512,256]{2,0,1:T(8,128)}), f32[8,512,256]{2,0,1:T(8,128)}, u32[]{:S(2)}, u32[]{:S(2)}) async-start(f32[8,512,256]{2,0,1:T(8,128)} %copy.63), calls=%async_computation | async-start | bytes 8388608 | tf_op jit(solution)/shard_map/all_to_all | solution.py:115
  18.6 1.2 exponential_select_fusion.2
  19.8 4.3 %fusion.11 = f32[8,1,128,128]{3,1,2,0:T(1,128)S(1)} fusion(f32[8,4,1,1]{1,2,3,0:T(1,128)S(1)} %copy.100, f32[8,4,128,128]{3,2,1,0:T(8,128)S(1)} %get-tuple-element.298), kind=kOutput, calls=%fused_computation.22 | convolution fusion | flops 6291456 | bytes 2621568 | tf_op jit(solution)/shard_map/lk,lkab->lab/dot_general | solution.py:54
  24.1 4.3 %fusion.7 = f32[8,1,128,128]{3,1,2,0:T(1,128)S(1)} fusion(f32[8,4,1,1]{1,2,3,0:T(1,128)S(1)} %copy.115, f32[8,4,128,128]{3,2,1,0:T(8,128)S(1)} %get-tuple-element.299), kind=kOutput, calls=%fused_computation.18 | convolution fusion | flops 6291456 | bytes 2621568 | tf_op jit(solution)/shard_map/lk,lkab->lab/dot_general | solution.py:54
  28.4 4.3 %fusion.13 = f32[8,1,128,128]{3,1,2,0:T(1,128)S(1)} fusion(f32[8,4,1,1]{1,2,3,0:T(1,128)S(1)} %copy.94, f32[8,4,128,128]{3,2,1,0:T(8,128)S(1)} %get-tuple-element.300), kind=kOutput, calls=%fused_computation.24 | convolution fusion | flops 6291456 | bytes 2621568 | tf_op jit(solution)/shard_map/lk,lkab->lab/dot_general | solution.py:54
  32.7 4.7 %fusion.9 = f32[8,1,128,128]{3,1,2,0:T(1,128)S(1)} fusion(f32[8,4,1,1]{1,2,3,0:T(1,128)S(1)} %copy.106, f32[8,4,128,128]{3,2,1,0:T(8,128)S(1)} %get-tuple-element.301), kind=kOutput, calls=%fused_computation.20 | convolution fusion | flops 6291456 | bytes 2621568 | tf_op jit(solution)/shard_map/lk,lkab->lab/dot_general | solution.py:54
  37.4 38.0 %all-to-all-done = f32[8,512,256]{2,0,1:T(8,128)} async-done(((f32[8,512,256]{2,0,1:T(8,128)}), f32[8,512,256]{2,0,1:T(8,128)}, u32[]{:S(2)}, u32[]{:S(2)}) %all-to-all-start) | async-done | bytes 4194336 | tf_op jit(solution)/shard_map/all_to_all | solution.py:115
  75.4 6.6 %copy.156 = f32[8,16,32,256]{3,1,2,0:T(8,128)} copy(f32[8,16,32,256]{3,0,2,1:T(8,128)} %bitcast.5) | data formatting | bytes 8388608 | tf_op jit(solution)/shard_map/all_to_all | solution.py:115
  82.0 4.8 %reshape.192 = f32[8,32,32,128]{3,2,1,0:T(8,128)} reshape(f32[8,32,16,256]{3,2,1,0:T(8,128)} %bitcast.178) | data formatting | bytes 8388608 | tf_op jit(solution)/shard_map/reshape | solution.py:86
  86.8 5.5 %fusion.136 = f32[8,128,32,32]{1,3,2,0:T(8,128)S(1)} fusion(f32[8,128,128,1]{2,1,3,0:T(8,128)S(1)} %bitcast.182, f32[8,32,32,128]{3,2,1,0:T(8,128)} %reshape.192), kind=kOutput, calls=%fused_computation.222 | convolution fusion | flops 1610612736 | bytes 8912896 | tf_op jit(solution)/shard_map/lab,lmcb->lmca/dot_general | solution.py:87
  92.4 16.3 %convolution_bitcast_fusion.1 = f32[8,32,4,32]{1,2,3,0:T(4,128)S(1)} fusion(f32[8,32,32,128]{3,2,1,0:T(8,128)S(1)} %copy-done.2, f32[128]{0:T(128)S(1)} %iota_subtract_fusion.9, f32[8,4]{1,0:T(8,128)S(1)} %copy.62, f32[8,4]{1,0:T(8,128)S(1)} %copy.65), kind=kOutput, calls=%fused_computation.31 | convolution fusion | flops 50339840 | bytes 4326144 | tf_op jit(solution)/shard_map/lkb,lmcb->lckm/dot_general | solution.py:88
  109.8 7.0 %bitcast_add_fusion.3 = f32[8,32,32,128]{3,2,1,0:T(8,128)S(1)} fusion(f32[8,128,32,32]{1,3,2,0:T(8,128)S(1)} %fusion.136, f32[8,32,4,32]{1,3,2,0:T(8,128)S(1)} %fusion.16, f32[128]{0:T(128)S(1)} %iota_add_fusion.1, f32[8,4]{1,0:T(8,128)S(1)} %copy.62, f32[8,4]{1,0:T(8,128)S(1)} %copy.70), kind=kOutput, calls=%fused_computation.14 | convolution fusion | flops 51388416 | bytes 8520448 | tf_op jit(solution)/shard_map/lak,lckm->lmca/dot_general | solution.py:102
  116.7 16.3 %convolution_bitcast_fusion = f32[8,32,4,32]{1,2,3,0:T(4,128)S(1)} fusion(f32[8,32,32,128]{3,2,1,0:T(8,128)S(1)} %bitcast_add_fusion.3, f32[8,4]{1,0:T(8,128)S(1)} %copy.73, f32[8,4]{1,0:T(8,128)S(1)} %copy.62), kind=kOutput, calls=%fused_computation.30 | convolution fusion | flops 50339840 | bytes 4325632 | tf_op jit(solution)/shard_map/lkb,lmcb->lckm/dot_general | solution.py:88
  133.0 4.6 %fusion.137 = f32[8,32,32,128]{3,2,1,0:T(8,128)S(1)} fusion(f32[8,32,32,128]{3,2,1,0:T(8,128)S(1)} %bitcast_add_fusion.3, f32[8,128,128,1]{2,1,3,0:T(8,128)S(1)} %bitcast.181), kind=kOutput, calls=%fused_computation.223 | convolution fusion | flops 1610612736 | bytes 8912896 | tf_op jit(solution)/shard_map/lab,lmcb->lmca/dot_general | solution.py:87
  138.7 8.4 %bitcast_add_fusion.2 = f32[8,32,32,128]{3,2,1,0:T(8,128)} fusion(f32[8,32,32,128]{3,2,1,0:T(8,128)S(1)} %fusion.137, f32[8,32,4,32]{1,3,2,0:T(8,128)S(1)} %fusion.15, f32[128]{0:T(128)S(1)} %iota_subtract_fusion.7, f32[8,4]{1,0:T(8,128)S(1)} %copy.62, f32[8,4]{1,0:T(8,128)S(1)} %copy.70), kind=kOutput, calls=%fused_computation.13 | convolution fusion | flops 51388416 | bytes 8520448 | tf_op jit(solution)/shard_map/lak,lckm->lmca/dot_general | solution.py:102
  147.1 5.0 %reshape.193 = f32[8,32,4096]{2,1,0:T(8,128)} reshape(f32[8,32,32,128]{3,2,1,0:T(8,128)} %bitcast_add_fusion.2) | data formatting | bytes 8388608 | tf_op jit(solution)/shard_map/reshape | solution.py:105
  152.1 2.9 fusion.2
  155.0 2.0 copy-done.3
  157.0 1.5 fusion.135
  158.4 5.7 %collective-permute-start = (f32[8,32,256]{2,1,0:T(8,128)}, f32[8,32,256]{2,1,0:T(8,128)S(1)}, u32[]{:S(2)}, u32[]{:S(2)}) collective-permute-start(f32[8,32,256]{2,1,0:T(8,128)} %get-tuple-element.295), channel_id=1, source_target_pairs={{0,240},{16,0},{32,16},{48,32},{64,48},{80,64},{96,80},{112,96},{1... | collective-permute-start | bytes 786440 | tf_op jit(solution)/shard_map/ppermute | solution.py:16
  164.8 22.2 %all-gather.3 = f32[16,8,4]{1,2,0:T(4,128)S(1)} all-gather(f32[1,8,4]{1,2,0:T(4,128)S(1)} %get-tuple-element.313), channel_id=2, replica_groups=mesh['row'=16,'col'=16] {'col'}, dimensions={0}, use_global_device_ids=true | all-gather | bytes 2176 | tf_op jit(solution)/shard_map/all_gather | solution.py:23
  187.0 4.3 %collective-permute-start.2 = (f32[8,32,256]{2,1,0:T(8,128)}, f32[8,32,256]{2,1,0:T(8,128)S(1)}, u32[]{:S(2)}, u32[]{:S(2)}) collective-permute-start(f32[8,32,256]{2,1,0:T(8,128)} %get-tuple-element.293), channel_id=1, source_target_pairs={{0,208},{16,224},{32,240},{48,0},{64,16},{80,32},{96,48},{112,64},... | collective-permute-start | bytes 786440 | tf_op jit(solution)/shard_map/ppermute | solution.py:16
  191.4 1.3 copy.89
  193.5 1.7 collective-permute-start.14
  195.2 1.8 collective-permute-start.3
  197.1 1.6 collective-permute-start.4
  198.7 2.7 collective-permute-start.5
  202.5 3.3 collective-permute-start.6
  205.9 5.1 %collective-permute-done.4 = f32[8,32,256]{2,1,0:T(8,128)S(1)} collective-permute-done((f32[8,32,256]{2,1,0:T(8,128)}, f32[8,32,256]{2,1,0:T(8,128)S(1)}, u32[]{:S(2)}, u32[]{:S(2)}) %collective-permute-start.4) | collective-permute-done | bytes 262176 | tf_op jit(solution)/shard_map/ppermute | solution.py:16
  212.0 5.8 %collective-permute-done.5 = f32[8,32,256]{2,1,0:T(8,128)S(1)} collective-permute-done((f32[8,32,256]{2,1,0:T(8,128)}, f32[8,32,256]{2,1,0:T(8,128)S(1)}, u32[]{:S(2)}, u32[]{:S(2)}) %collective-permute-start.5) | collective-permute-done | bytes 262176 | tf_op jit(solution)/shard_map/ppermute | solution.py:16
  218.6 4.4 %collective-permute-done.6 = f32[8,32,256]{2,1,0:T(8,128)S(1)} collective-permute-done((f32[8,32,256]{2,1,0:T(8,128)}, f32[8,32,256]{2,1,0:T(8,128)S(1)}, u32[]{:S(2)}, u32[]{:S(2)}) %collective-permute-start.6) | collective-permute-done | bytes 262176 | tf_op jit(solution)/shard_map/ppermute | solution.py:16
  223.0 2.9 collective-permute-start.9
  226.0 15.3 %collective-permute-start.10 = (f32[8,32,256]{2,1,0:T(8,128)S(1)}, f32[8,32,256]{2,1,0:T(8,128)S(1)}, u32[]{:S(2)}, u32[]{:S(2)}) collective-permute-start(f32[8,32,256]{2,1,0:T(8,128)S(1)} %get-tuple-element.285), channel_id=1, source_target_pairs={{0,80},{16,96},{32,112},{48,128},{64,144},{80,160},{96,176},{112,1... | collective-permute-start | bytes 786440 | tf_op jit(solution)/shard_map/ppermute | solution.py:16
  241.5 5.9 %collective-permute-start.12 = (f32[8,32,256]{2,1,0:T(8,128)S(1)}, f32[8,32,256]{2,1,0:T(8,128)S(1)}, u32[]{:S(2)}, u32[]{:S(2)}) collective-permute-start(f32[8,32,256]{2,1,0:T(8,128)S(1)} %get-tuple-element.283), channel_id=1, source_target_pairs={{0,48},{16,64},{32,80},{48,96},{64,112},{80,128},{96,144},{112,160... | collective-permute-start | bytes 786440 | tf_op jit(solution)/shard_map/ppermute | solution.py:16
  247.4 6.1 %collective-permute-done.10 = f32[8,32,256]{2,1,0:T(8,128)S(1)} collective-permute-done((f32[8,32,256]{2,1,0:T(8,128)S(1)}, f32[8,32,256]{2,1,0:T(8,128)S(1)}, u32[]{:S(2)}, u32[]{:S(2)}) %collective-permute-start.10) | collective-permute-done | bytes 262176 | tf_op jit(solution)/shard_map/ppermute | solution.py:16
  253.5 1.7 collective-permute-done.11
  258.1 2.0 copy-done
  260.1 2.3 convolution_bitcast_fusion.6
  262.8 27.3 %all-gather.1 = f32[128,4,256]{2,1,0:T(4,128)S(1)} all-gather(f32[8,4,256]{2,1,0:T(4,128)S(1)} %bitcast.186), channel_id=3, replica_groups=mesh['row'=16,'col'=16] {'col'}, dimensions={0}, use_global_device_ids=true | all-gather | bytes 557056 | tf_op jit(solution)/shard_map/all_gather | solution.py:23
  290.1 3.3 while.28
  293.9 6.7 %fusion.41 = f32[8,4,256,128]{3,2,1,0:T(8,128)S(1)} fusion(f32[8,4,4,256]{3,1,2,0:T(4,128)S(1)} %fusion.18, f32[8,4]{1,0:T(8,128)S(1)} %copy.76, f32[8,4]{1,0:T(8,128)S(1)} %copy.85, f32[128]{0:T(128)S(1)} %copy-done.20), kind=kOutput, calls=%fused_computation.63 | convolution fusion | flops 50339840 | bytes 4326144 | tf_op jit(solution)/shard_map/lak,lckm->lcam/dot_general | solution.py:104
  300.6 6.9 %convolution_add_fusion = f32[8,4,256,128]{3,2,1,0:T(8,128)S(1)} fusion(f32[8,4,256,128]{3,2,1,0:T(8,128)S(1)} %fusion.41, f32[8,4,128,256]{3,2,1,0:T(8,128)S(1)} %bitcast.177, f32[8,128,128,1]{2,1,3,0:T(8,128)S(1)} %bitcast.180), kind=kOutput, calls=%fused_computation.17 | convolution fusion | flops 1611661312 | bytes 13107200 | tf_op jit(solution)/shard_map/lab,lcbm->lcam/dot_general | solution.py:91
  307.6 3.6 %fusion.19 = f32[8,4,4,256]{3,2,1,0:T(4,128)S(1)} fusion(f32[8,4,256,128]{3,2,1,0:T(8,128)S(1)} %convolution_add_fusion, f32[8,4]{1,0:T(8,128)S(1)} %copy-done.8, f32[8,4]{1,0:T(8,128)S(1)} %copy.76), kind=kOutput, calls=%fused_computation.40 | convolution fusion | flops 50339840 | bytes 4325632 | tf_op jit(solution)/shard_map/lkb,lcbm->lckm/dot_general | solution.py:92
  311.2 5.9 %fusion.5 = f32[8,4,256,128]{2,3,1,0:T(8,128)} fusion(f32[8,128,128,1]{2,1,3,0:T(8,128)S(1)} %bitcast.179, f32[8,4,256,128]{3,2,1,0:T(8,128)S(1)} %convolution_add_fusion), kind=kOutput, calls=%fused_computation.11 | convolution fusion | flops 1610612736 | bytes 8912896 | tf_op jit(solution)/shard_map/lab,lcbm->lcam/dot_general | solution.py:91
  317.5 17.4 %all-gather.2 = f32[128,4,256]{2,1,0:T(4,128)S(1)} all-gather(f32[8,4,256]{2,1,0:T(4,128)S(1)} %bitcast.187), channel_id=4, replica_groups=mesh['row'=16,'col'=16] {'col'}, dimensions={0}, use_global_device_ids=true | all-gather | bytes 557056 | tf_op jit(solution)/shard_map/all_gather | solution.py:23
  334.9 3.1 while.29
  338.5 7.5 %add_exponential_fusion = f32[8,4,256,128]{2,3,1,0:T(8,128)} fusion(f32[8,4,256,128]{2,3,1,0:T(8,128)} %fusion.5, f32[8,4,4,256]{3,1,2,0:T(4,128)S(1)} %fusion.17, f32[8,4]{1,0:T(8,128)S(1)} %copy.76, f32[8,4]{1,0:T(8,128)S(1)} %copy.85, f32[128]{0:T(128)S(1)} %copy-done.18), kind=kOutput, calls=%fused_computation.16 | convolution fusion | flops 51388416 | bytes 8520448 | tf_op jit(solution)/shard_map/lak,lckm->lcam/dot_general | solution.py:104
  (225 shorter events, 20.4 us)
Async XLA Ops:
  6.6 8.0 %copy-start.10 = (f32[8,4]{0,1:T(4,128)S(1)}, f32[8,4]{0,1:T(4,128)}, u32[]{:S(2)}) copy-start(f32[8,4]{0,1:T(4,128)} %param.11) | copy-start | bytes 388
  6.6 8.1 %copy-start.16 = (f32[8,4]{0,1:T(4,128)S(1)}, f32[8,4]{0,1:T(4,128)}, u32[]{:S(2)}) copy-start(f32[8,4]{0,1:T(4,128)} %param.10) | copy-start | bytes 388
  6.6 8.6 %copy-start.9 = (f32[8,4]{0,1:T(4,128)S(1)}, f32[8,4]{0,1:T(4,128)}, u32[]{:S(2)}) copy-start(f32[8,4]{0,1:T(4,128)} %param.13) | copy-start | bytes 388
  6.6 8.6 %copy-start.13 = (f32[8,4]{0,1:T(4,128)S(1)}, f32[8,4]{0,1:T(4,128)}, u32[]{:S(2)}) copy-start(f32[8,4]{0,1:T(4,128)} %param.12) | copy-start | bytes 388
  6.6 68.8 %all-to-all-start = ((f32[8,512,256]{2,0,1:T(8,128)}), f32[8,512,256]{2,0,1:T(8,128)}, u32[]{:S(2)}, u32[]{:S(2)}) async-start(f32[8,512,256]{2,0,1:T(8,128)} %copy.63), calls=%async_computation | async-start | bytes 8388608 | tf_op jit(solution)/shard_map/all_to_all | solution.py:115
  16.2 76.2 %copy-start.11 = (f32[128]{0:T(128)}, f32[128]{0:T(128)S(1)}, u32[]{:S(2)}) copy-start(f32[128]{0:T(128)S(1)} %iota_subtract_fusion.9) | copy-start | bytes 1540
  16.2 93.6 %copy-start.19 = (f32[128]{0:T(128)}, f32[128]{0:T(128)S(1)}, u32[]{:S(2)}) copy-start(f32[128]{0:T(128)S(1)} %iota_add_fusion.1) | copy-start | bytes 1540
  16.2 122.5 %copy-start.17 = (f32[128]{0:T(128)}, f32[128]{0:T(128)S(1)}, u32[]{:S(2)}) copy-start(f32[128]{0:T(128)S(1)} %iota_subtract_fusion.7) | copy-start | bytes 1540
  86.8 5.6 %copy-start.2 = (f32[8,32,32,128]{3,2,1,0:T(8,128)S(1)}, f32[8,32,32,128]{3,2,1,0:T(8,128)}, u32[]{:S(2)}) copy-start(f32[8,32,32,128]{3,2,1,0:T(8,128)} %reshape.192) | copy-start | bytes 12582916
  155.0 2.0 copy-start.3
  158.4 38.6 %collective-permute-start.1 = (f32[8,32,256]{2,1,0:T(8,128)}, f32[8,32,256]{2,1,0:T(8,128)S(1)}, u32[]{:S(2)}, u32[]{:S(2)}) collective-permute-start(f32[8,32,256]{2,1,0:T(8,128)} %get-tuple-element.294), channel_id=1, source_target_pairs={{0,224},{16,240},{32,0},{48,16},{64,32},{80,48},{96,64},{112,80},{... | collective-permute-start | bytes 786440 | tf_op jit(solution)/shard_map/ppermute | solution.py:16
  158.4 36.8 %collective-permute-start = (f32[8,32,256]{2,1,0:T(8,128)}, f32[8,32,256]{2,1,0:T(8,128)S(1)}, u32[]{:S(2)}, u32[]{:S(2)}) collective-permute-start(f32[8,32,256]{2,1,0:T(8,128)} %get-tuple-element.295), channel_id=1, source_target_pairs={{0,240},{16,0},{32,16},{48,32},{64,48},{80,64},{96,80},{112,96},{1... | collective-permute-start | bytes 786440 | tf_op jit(solution)/shard_map/ppermute | solution.py:16
  187.0 11.6 %collective-permute-start.2 = (f32[8,32,256]{2,1,0:T(8,128)}, f32[8,32,256]{2,1,0:T(8,128)S(1)}, u32[]{:S(2)}, u32[]{:S(2)}) collective-permute-start(f32[8,32,256]{2,1,0:T(8,128)} %get-tuple-element.293), channel_id=1, source_target_pairs={{0,208},{16,224},{32,240},{48,0},{64,16},{80,32},{96,48},{112,64},... | collective-permute-start | bytes 786440 | tf_op jit(solution)/shard_map/ppermute | solution.py:16
  193.5 61.9 %collective-permute-start.14 = (f32[8,32,256]{2,1,0:T(8,128)S(1)}, f32[8,32,256]{2,1,0:T(8,128)S(1)}, u32[]{:S(2)}, u32[]{:S(2)}) collective-permute-start(f32[8,32,256]{2,1,0:T(8,128)S(1)} %get-tuple-element.281), channel_id=1, source_target_pairs={{0,16},{16,32},{32,48},{48,64},{64,80},{80,96},{96,112},{112,128},... | collective-permute-start | bytes 786440 | tf_op jit(solution)/shard_map/ppermute | solution.py:16
  195.2 60.1 %collective-permute-start.13 = (f32[8,32,256]{2,1,0:T(8,128)S(1)}, f32[8,32,256]{2,1,0:T(8,128)S(1)}, u32[]{:S(2)}, u32[]{:S(2)}) collective-permute-start(f32[8,32,256]{2,1,0:T(8,128)S(1)} %get-tuple-element.282), channel_id=1, source_target_pairs={{0,32},{16,48},{32,64},{48,80},{64,96},{80,112},{96,128},{112,144}... | collective-permute-start | bytes 786440 | tf_op jit(solution)/shard_map/ppermute | solution.py:16
  195.2 7.3 %collective-permute-start.3 = (f32[8,32,256]{2,1,0:T(8,128)}, f32[8,32,256]{2,1,0:T(8,128)S(1)}, u32[]{:S(2)}, u32[]{:S(2)}) collective-permute-start(f32[8,32,256]{2,1,0:T(8,128)} %get-tuple-element.292), channel_id=1, source_target_pairs={{0,192},{16,208},{32,224},{48,240},{64,0},{80,16},{96,32},{112,48}... | collective-permute-start | bytes 786440 | tf_op jit(solution)/shard_map/ppermute | solution.py:16
  197.1 13.9 %collective-permute-start.4 = (f32[8,32,256]{2,1,0:T(8,128)}, f32[8,32,256]{2,1,0:T(8,128)S(1)}, u32[]{:S(2)}, u32[]{:S(2)}) collective-permute-start(f32[8,32,256]{2,1,0:T(8,128)} %get-tuple-element.291), channel_id=1, source_target_pairs={{0,176},{16,192},{32,208},{48,224},{64,240},{80,0},{96,16},{112,32... | collective-permute-start | bytes 786440 | tf_op jit(solution)/shard_map/ppermute | solution.py:16
  198.7 19.2 %collective-permute-start.5 = (f32[8,32,256]{2,1,0:T(8,128)}, f32[8,32,256]{2,1,0:T(8,128)S(1)}, u32[]{:S(2)}, u32[]{:S(2)}) collective-permute-start(f32[8,32,256]{2,1,0:T(8,128)} %get-tuple-element.290), channel_id=1, source_target_pairs={{0,160},{16,176},{32,192},{48,208},{64,224},{80,240},{96,0},{112,1... | collective-permute-start | bytes 786440 | tf_op jit(solution)/shard_map/ppermute | solution.py:16
  202.5 20.5 %collective-permute-start.6 = (f32[8,32,256]{2,1,0:T(8,128)}, f32[8,32,256]{2,1,0:T(8,128)S(1)}, u32[]{:S(2)}, u32[]{:S(2)}) collective-permute-start(f32[8,32,256]{2,1,0:T(8,128)} %get-tuple-element.289), channel_id=1, source_target_pairs={{0,144},{16,160},{32,176},{48,192},{64,208},{80,224},{96,240},{112... | collective-permute-start | bytes 786440 | tf_op jit(solution)/shard_map/ppermute | solution.py:16
  211.0 15.0 %collective-permute-start.7 = (f32[8,32,256]{2,1,0:T(8,128)}, f32[8,32,256]{2,1,0:T(8,128)S(1)}, u32[]{:S(2)}, u32[]{:S(2)}) collective-permute-start(f32[8,32,256]{2,1,0:T(8,128)} %get-tuple-element.288), channel_id=1, source_target_pairs={{0,128},{16,144},{32,160},{48,176},{64,192},{80,208},{96,224},{112... | collective-permute-start | bytes 786440 | tf_op jit(solution)/shard_map/ppermute | solution.py:16
  217.8 23.5 %collective-permute-start.8 = (f32[8,32,256]{2,1,0:T(8,128)}, f32[8,32,256]{2,1,0:T(8,128)S(1)}, u32[]{:S(2)}, u32[]{:S(2)}) collective-permute-start(f32[8,32,256]{2,1,0:T(8,128)} %get-tuple-element.287), channel_id=1, source_target_pairs={{0,112},{16,128},{32,144},{48,160},{64,176},{80,192},{96,208},{112... | collective-permute-start | bytes 786440 | tf_op jit(solution)/shard_map/ppermute | solution.py:16
  223.0 18.5 %collective-permute-start.9 = (f32[8,32,256]{2,1,0:T(8,128)S(1)}, f32[8,32,256]{2,1,0:T(8,128)S(1)}, u32[]{:S(2)}, u32[]{:S(2)}) collective-permute-start(f32[8,32,256]{2,1,0:T(8,128)S(1)} %get-tuple-element.286), channel_id=1, source_target_pairs={{0,96},{16,112},{32,128},{48,144},{64,160},{80,176},{96,192},{112,... | collective-permute-start | bytes 786440 | tf_op jit(solution)/shard_map/ppermute | solution.py:16
  226.0 27.5 %collective-permute-start.10 = (f32[8,32,256]{2,1,0:T(8,128)S(1)}, f32[8,32,256]{2,1,0:T(8,128)S(1)}, u32[]{:S(2)}, u32[]{:S(2)}) collective-permute-start(f32[8,32,256]{2,1,0:T(8,128)S(1)} %get-tuple-element.285), channel_id=1, source_target_pairs={{0,80},{16,96},{32,112},{48,128},{64,144},{80,160},{96,176},{112,1... | collective-permute-start | bytes 786440 | tf_op jit(solution)/shard_map/ppermute | solution.py:16
  241.4 13.9 %collective-permute-start.11 = (f32[8,32,256]{2,1,0:T(8,128)S(1)}, f32[8,32,256]{2,1,0:T(8,128)S(1)}, u32[]{:S(2)}, u32[]{:S(2)}) collective-permute-start(f32[8,32,256]{2,1,0:T(8,128)S(1)} %get-tuple-element.284), channel_id=1, source_target_pairs={{0,64},{16,80},{32,96},{48,112},{64,128},{80,144},{96,160},{112,17... | collective-permute-start | bytes 786440 | tf_op jit(solution)/shard_map/ppermute | solution.py:16
  241.5 13.8 %collective-permute-start.12 = (f32[8,32,256]{2,1,0:T(8,128)S(1)}, f32[8,32,256]{2,1,0:T(8,128)S(1)}, u32[]{:S(2)}, u32[]{:S(2)}) collective-permute-start(f32[8,32,256]{2,1,0:T(8,128)S(1)} %get-tuple-element.283), channel_id=1, source_target_pairs={{0,48},{16,64},{32,80},{48,96},{64,112},{80,128},{96,144},{112,160... | collective-permute-start | bytes 786440 | tf_op jit(solution)/shard_map/ppermute | solution.py:16
  257.8 2.3 copy-start.12
  258.1 2.0 copy-start
  258.1 4.3 %copy-start.7 = (f32[8,4,4]{2,1,0:T(4,128)S(1)}, f32[8,4,4]{2,1,0:T(4,128)}, u32[]{:S(2)}) copy-start(f32[8,4,4]{2,1,0:T(4,128)} %get-tuple-element.305) | copy-start | bytes 1540
  258.1 35.3 %copy-start.6 = (f32[8,4,4]{1,2,0:T(4,128)S(1)}, f32[8,4,4]{1,2,0:T(4,128)}, u32[]{:S(2)}) copy-start(f32[8,4,4]{1,2,0:T(4,128)} %get-tuple-element.303) | copy-start | bytes 1540
  258.1 35.3 %copy-start.15 = (f32[4,4]{1,0:T(4,128)S(1)}, f32[4,4]{1,0:T(4,128)}, u32[]{:S(2)}) copy-start(f32[4,4]{1,0:T(4,128)} %get-tuple-element.326) | copy-start | bytes 196
  258.1 35.3 %copy-start.22 = (pred[4,4]{1,0:T(4,128)(4,1)S(1)}, pred[4,4]{1,0:T(4,128)(4,1)}, u32[]{:S(2)}) copy-start(pred[4,4]{1,0:T(4,128)(4,1)} %get-tuple-element.324) | copy-start | bytes 52
  258.1 35.7 %copy-start.20 = (f32[128]{0:T(128)S(1)}, f32[128]{0:T(128)}, u32[]{:S(2)}) copy-start(f32[128]{0:T(128)} %copy-done.19) | copy-start | bytes 1540
  293.4 7.2 %copy-start.1 = (f32[8,512,256]{2,1,0:T(8,128)S(1)}, f32[8,512,256]{2,1,0:T(8,128)}, u32[]{:S(2)}) copy-start(f32[8,512,256]{2,1,0:T(8,128)} %copy-done) | copy-start | bytes 12582916
  300.6 7.0 %copy-start.8 = (f32[8,4]{1,0:T(8,128)S(1)}, f32[8,4]{1,0:T(8,128)}, u32[]{:S(2)}) copy-start(f32[8,4]{1,0:T(8,128)} %copy.89) | copy-start | bytes 388
  311.2 5.9 %copy-start.5 = (f32[8,4,4]{2,1,0:T(4,128)S(1)}, f32[8,4,4]{2,1,0:T(4,128)}, u32[]{:S(2)}) copy-start(f32[8,4,4]{2,1,0:T(4,128)} %get-tuple-element.304) | copy-start | bytes 1540
  311.2 26.9 %copy-start.4 = (f32[8,4,4]{1,2,0:T(4,128)S(1)}, f32[8,4,4]{1,2,0:T(4,128)}, u32[]{:S(2)}) copy-start(f32[8,4,4]{1,2,0:T(4,128)} %get-tuple-element.302) | copy-start | bytes 1540
  311.2 26.9 %copy-start.14 = (f32[4,4]{1,0:T(4,128)S(1)}, f32[4,4]{1,0:T(4,128)}, u32[]{:S(2)}) copy-start(f32[4,4]{1,0:T(4,128)} %get-tuple-element.325) | copy-start | bytes 196
  311.2 26.9 %copy-start.21 = (pred[4,4]{1,0:T(4,128)(4,1)S(1)}, pred[4,4]{1,0:T(4,128)(4,1)}, u32[]{:S(2)}) copy-start(pred[4,4]{1,0:T(4,128)(4,1)} %get-tuple-element.323) | copy-start | bytes 52
  311.2 27.3 %copy-start.18 = (f32[128]{0:T(128)S(1)}, f32[128]{0:T(128)}, u32[]{:S(2)}) copy-start(f32[128]{0:T(128)} %copy-done.17) | copy-start | bytes 1540
